TPU v7x, 256 devices: a whole 4x4x8 slice. The times are simulated.
256 devices in a mesh: dp: 8 (over x, y_hi), tm: 32 (over y_lo, z, core).
Axes of the slice: x: 4, y: 4 (y_hi: 2, y_lo: 2; y = y_hi * 2 + y_lo), z: 8, core: 2. Of those that a mesh axis runs over, the one named last changes fastest.
Arguments:
- qkv: bfloat16 [8, 3, 12544, 1536], P('dp', None, 'tm'), may hold values from -12 to 12
- w_out: bfloat16 [1536, 1536], P('dp'), may hold values from -0.15625 to 0.15625
- d_out: bfloat16 [8, 12544, 1536], P('dp', 'tm'), may hold values from -6 to 6
- clip_ids: int32 [8, 256], P('dp'), may hold values from 0 to 3, never falling along the last dimension, each value on 1 to 128 neighbouring positions
Outputs:
- mixed: bfloat16 [8, 12544, 1536], P('dp', 'tm')
- d_qkv: bfloat16 [8, 3, 12544, 1536], P('dp', None, 'tm')
- d_weight: float32 [1536, 1536], P('tm', 'dp')
Inputs may be any that keep to these rules, and one draw needn't show every extreme that they name: `clip_ids`: clip numbers never fall along the frames of a sequence; a clip spans at most half of the 256 frames.
All inputs are finite; a program needn't handle non-finite values.
Results may differ from a plain program's by a relative error of at most 0.0065.
Values may be sent and summed in bfloat16 or wider, within the bound.
A program may use at most 192 MiB of HBM per device.

v0:
```python
import math

import jax
import jax.numpy as jnp
from jax import lax
from jax.sharding import PartitionSpec as P

HEADS = 24
HEAD_DIM = 64
WIN_T = 8
SPATIAL = 49
SHIFT = 4


NEG_FILL = -1e30


def from_behind(value, axis, steps):
    count = lax.axis_size(axis)
    pairs = [(source, (source + steps) % count) for source in range(count)]
    return lax.ppermute(value, axis, pairs)


def window_pass(queries, keys_in, values, attn_cot, allowed):
    score_scale = HEAD_DIM ** (-0.5)
    scores = (
        jnp.einsum("wqge,wkge->wgqk", queries, keys_in, preferred_element_type=jnp.float32)
        * score_scale
    )
    scores = jnp.where(allowed[:, None], scores, NEG_FILL)
    row_max = jnp.max(scores, axis=-1, keepdims=True)
    exp_scores = jnp.exp(scores - row_max)
    attn_probs = exp_scores / jnp.sum(exp_scores, axis=-1, keepdims=True)
    probs_low = attn_probs.astype(jnp.bfloat16)
    attended = jnp.einsum(
        "wgqk,wkge->wqge", probs_low, values, preferred_element_type=jnp.float32
    ).astype(jnp.bfloat16)
    grad_probs = jnp.einsum("wqge,wkge->wgqk", attn_cot, values, preferred_element_type=jnp.float32)
    row_total = jnp.sum(attn_probs * grad_probs, axis=-1, keepdims=True)
    grad_scores = (attn_probs * (grad_probs - row_total)).astype(jnp.bfloat16)
    grad_query = (
        jnp.einsum("wgqk,wkge->wqge", grad_scores, keys_in, preferred_element_type=jnp.float32)
        * score_scale
    ).astype(jnp.bfloat16)
    grad_keys = (
        jnp.einsum("wgqk,wqge->wkge", grad_scores, queries, preferred_element_type=jnp.float32)
        * score_scale
    )
    grad_values = jnp.einsum(
        "wgqk,wqge->wkge", probs_low, attn_cot, preferred_element_type=jnp.float32
    )
    return (attended, grad_query, grad_keys, grad_values)


def to_groups(stacked):
    return stacked.reshape(stacked.shape[0], stacked.shape[1], HEADS // 2, 2, HEAD_DIM).transpose(
        2, 0, 1, 3, 4
    )


def join_groups(grouped):
    return grouped.transpose(1, 2, 0, 3, 4).reshape(grouped.shape[1] * grouped.shape[2], -1)


def clip_of(frame_glob, clip_row):
    total_frames = clip_row.shape[0]
    matches = frame_glob[:, None] == jnp.arange(total_frames, dtype=jnp.int32)[None, :]
    return jnp.sum(jnp.where(matches, clip_row[None, :], 0), axis=1)


def run_windows(rolled, rolled_cot, frame_ids):
    win_count = rolled.shape[1] // (WIN_T * SPATIAL)
    win_tok = WIN_T * SPATIAL
    token_ids = jnp.repeat(frame_ids, SPATIAL).reshape(win_count, win_tok)
    allowed = token_ids[:, :, None] == token_ids[:, None, :]

    def per_group(operands):
        return window_pass(operands[0], operands[1], operands[2], operands[3], allowed)

    def shaped(tokens_d):
        return to_groups(tokens_d.reshape(win_count, win_tok, -1))

    results = lax.map(
        per_group, (shaped(rolled[0]), shaped(rolled[1]), shaped(rolled[2]), shaped(rolled_cot))
    )
    attended = join_groups(results[0])
    grads = jnp.stack(
        [
            join_groups(results[1]),
            join_groups(results[2]).astype(jnp.bfloat16),
            join_groups(results[3]).astype(jnp.bfloat16),
        ]
    )
    return (attended, grads)


def per_device(qkv, w_out, d_out, clip_ids):
    tok_count = qkv.shape[2]
    frames_dev = tok_count // SPATIAL
    edge_tok = SHIFT * SPATIAL
    cot_in = d_out[0]
    transposed_dims = (((1,), (1,)), ((), ()))
    attn_cot = lax.dot_general(
        cot_in,
        lax.all_gather(w_out, "dp", axis=0, tiled=True),
        transposed_dims,
        preferred_element_type=jnp.float32,
    ).astype(jnp.bfloat16)
    from_next = from_behind(qkv[0, :, :edge_tok], "tm", -1)
    rolled = jnp.concatenate([qkv[0, :, edge_tok:], from_next], axis=1)
    cot_next = from_behind(attn_cot[:edge_tok], "tm", -1)
    rolled_cot = jnp.concatenate([attn_cot[edge_tok:], cot_next], axis=0)
    total_frames = clip_ids.shape[1]
    first_frame = lax.axis_index("tm") * frames_dev + SHIFT
    frame_glob = (first_frame + jnp.arange(frames_dev, dtype=jnp.int32)) % total_frames
    frame_ids = clip_of(frame_glob, clip_ids[0])
    attended, grads = run_windows(rolled, rolled_cot, frame_ids)
    tails = jnp.concatenate([attended[None, -edge_tok:], grads[:, -edge_tok:]], axis=0)
    from_prev = from_behind(tails, "tm", 1)
    attended = jnp.concatenate([from_prev[0], attended[:-edge_tok]], axis=0)
    grads = jnp.concatenate([from_prev[1:], grads[:, :-edge_tok]], axis=1)
    mixed = jnp.dot(
        attended,
        lax.all_gather(w_out, "dp", axis=0, tiled=True),
        preferred_element_type=jnp.float32,
    ).astype(jnp.bfloat16)
    norm_factor = 1.0 / math.sqrt(lax.axis_size("dp") * lax.axis_size("tm") * tok_count)
    leading_dims = (((0,), (0,)), ((), ()))
    partial_rows = lax.psum_scatter(
        lax.dot_general(attended, cot_in, leading_dims, preferred_element_type=jnp.float32),
        "tm",
        scatter_dimension=0,
        tiled=True,
    )
    grad_block = lax.psum_scatter(partial_rows, "dp", scatter_dimension=1, tiled=True)
    return (mixed[None], grads[None], grad_block * norm_factor)


def solution(mesh):
    return jax.shard_map(
        per_device,
        mesh=mesh,
        in_specs=(P("dp", None, "tm", None), P("dp", None), P("dp", "tm", None), P("dp", None)),
        out_specs=(P("dp", "tm", None), P("dp", None, "tm", None), P("tm", "dp")),
        check_vma=False,
    )
```

profile of v0, /device:TPU:10, one launch (start us, length us, event | category | flops | bytes accessed | tf_op | source)
XLA Modules:
  0.0 547.5 jit_solution(10505011367443203232)
XLA Ops:
  8.0 3.7 slice_bitcast_fusion
  11.6 5.2 collective-permute-start
  16.8 83.5 %all-gather.2.cloned.1.call-done = bf16[1536,1536]{1,0:T(8,128)(2,1)} async-done(((bf16[192,1536]{1,0:T(8,128)(2,1)}), bf16[1536,1536]{1,0:T(8,128)(2,1)}) %all-gather.2.cloned.1.call-update) | async-done | bytes 4718608 | tf_op jit(solution)/shard_map/all_gather | solution.py:105
  100.3 4.4 convolution_convert_fusion.2
  105.9 3.2 collective-permute-start.1
  109.5 3.2 pad_maximum_fusion.3
  122.1 157.1 %while.17 = (s32[]{:T(128)}, bf16[12,1,392,2,64]{2,4,3,1,0:T(8,128)(2,1)}, bf16[12,1,392,2,64]{2,4,3,1,0:T(8,128)(2,1)}, bf16[12,1,392,2,64]{2,4,3,1,0:T(8,128)(...) while((s32[]{:T(128)}, ...), condition=%wide.region_5.6_spmd.clone, body=%wide.region_1.5_spmd.clone.sunk | while | flops 321514080 | bytes 10996309 | solution.py:83
  137.2 2.7 fusion.123
  140.0 2.7 fusion.120
  150.3 2.7 fusion.123
  153.1 2.7 fusion.120
  166.2 2.7 fusion.120
  176.6 2.7 fusion.123
  189.7 2.7 fusion.123
  202.7 2.7 fusion.123
  228.9 2.7 fusion.123
  231.7 2.7 fusion.120
  242.0 2.7 fusion.123
  255.1 2.7 fusion.123
  257.8 2.7 fusion.120
  268.2 2.7 fusion.123
  283.6 2.8 fusion.81
  288.6 5.8 %copy.52 = bf16[4,196,1536]{2,0,1:T(4,128)(2,1)} copy(bf16[4,196,1536]{1,2,0:T(8,128)(2,1)} %pad_maximum_fusion.1) | data formatting | bytes 4816896 | tf_op jit(solution)/shard_map/concatenate | solution.py:118
  294.3 31.1 %collective-permute-done.2 = bf16[4,196,1536]{2,0,1:T(4,128)(2,1)S(1)} collective-permute-done((bf16[4,196,1536]{2,0,1:T(4,128)(2,1)}, bf16[4,196,1536]{2,0,1:T(4,128)(2,1)S(1)}, u32[]{:S(2)}, u32[]{:S(2)}) %collective-permute-start.2) | collective-permute-done | bytes 2408480 | tf_op jit(solution)/shard_map/ppermute | solution.py:21
  329.8 6.6 %fusion.71 = f32[1536,1536]{1,0:T(8,128)} fusion(bf16[1,392,1536]{2,1,0:T(8,128)(2,1)S(1)} %copy-done, bf16[196,1536]{0,1:T(8,128)(2,1)S(1)} %bitcast.181, bf16[196,1536]{0,1:T(8,128)(2,1)} %bitcast.183), kind=kOutput, calls=%fused_computation.71 | convolution fusion | flops 1852096512 | bytes 11845632 | tf_op jit(solution)/shard_map/dot_general | solution.py:130
  336.8 4.4 slice.67
  341.1 5.5 %copy.63 = bf16[3,196,1536]{1,2,0:T(8,128)(2,1)} copy(bf16[3,196,1536]{2,0,1:T(4,128)(2,1)} %slice.67) | data formatting | bytes 3612672
  346.6 116.2 %reduce-scatter.5.cloned.1.call-done = f32[48,1536]{1,0:T(8,128)} async-done(((f32[1536,1536]{1,0:T(8,128)}), f32[48,1536]{1,0:T(8,128)}) %reduce-scatter.5.cloned.1.call-update) | async-done | bytes 294928 | tf_op jit(solution)/shard_map/reduce_scatter | solution.py:129
  465.0 6.4 %maximum_bitcast_fusion = bf16[1,3,392,1536]{2,3,1,0:T(8,128)(2,1)} fusion(bf16[3,196,1536]{1,2,0:T(8,128)(2,1)} %get-tuple-element.148, bf16[3,196,1536]{1,2,0:T(8,128)(2,1)} %copy.63), kind=kLoop, calls=%fused_computation.55 | loop fusion | flops 7225344 | bytes 7225344 | tf_op jit(solution)/shard_map/broadcast_in_dim | solution.py:136
  471.4 6.3 %copy.55 = bf16[1,3,392,1536]{3,2,1,0:T(8,128)(2,1)} copy(bf16[1,3,392,1536]{2,3,1,0:T(8,128)(2,1)} %maximum_bitcast_fusion) | data formatting | bytes 7225344
  477.7 5.6 %fusion.68 = bf16[1,392,1536]{2,1,0:T(8,128)(2,1)} fusion(bf16[1536,1536]{1,0:T(8,128)(2,1)} %all-gather.2.cloned.1.call-done, bf16[196,1536]{0,1:T(8,128)(2,1)S(1)} %bitcast.182, bf16[196,1536]{0,1:T(8,128)(2,1)S(1)} %bitcast.184), kind=kOutput, calls=%fused_computation.63 | convolution fusion | flops 1852698624 | bytes 7127040 | tf_op jit(solution)/shard_map/dot_general | solution.py:122
  483.3 56.1 %reduce-scatter.7.cloned.1.call-done = f32[192,48]{1,0:T(8,128)} async-done(((f32[1536,48]{1,0:T(8,128)}), f32[192,48]{1,0:T(8,128)}) %reduce-scatter.7.cloned.1.call-update) | async-done | bytes 36880
  (129 shorter events, 145.4 us)
Async XLA Ops:
  7.2 93.1 %copy-start = (bf16[1,392,1536]{2,1,0:T(8,128)(2,1)S(1)}, bf16[1,392,1536]{2,1,0:T(8,128)(2,1)}, u32[]{:S(2)}) copy-start(bf16[1,392,1536]{2,1,0:T(8,128)(2,1)} %param.8) | copy-start | bytes 3612676
  7.2 93.1 %all-gather.2.cloned.1.call-start = ((), (), s32[]{:S(2)}) async-start(), calls=%async_computation.2 | async-start | bytes 5308416 | tf_op jit(solution)/shard_map/all_gather | solution.py:105
  7.9 454.9 %reduce-scatter.5.cloned.1.call-start = ((), (), s32[]{:S(2)}) async-start(), calls=%async_computation.3 | async-start | bytes 9732096 | tf_op jit(solution)/shard_map/reduce_scatter | solution.py:129
  11.6 97.8 %collective-permute-start = (bf16[3,196,1536]{2,1,0:T(8,128)(2,1)}, bf16[3,196,1536]{2,1,0:T(8,128)(2,1)}, u32[]{:S(2)}, u32[]{:S(2)}) collective-permute-start(bf16[3,196,1536]{2,1,0:T(8,128)(2,1)} %get-tuple-element.153), channel_id=1, source_target_pairs={{0,31},{1,0},{2,1},{3,2},{4,3},{5,4},{6,5},{7,6},{8,7},{9,8},{10,9... | collective-permute-start | bytes 5419016 | tf_op jit(solution)/shard_map/ppermute | solution.py:21
  104.7 4.4 copy-start.7
  105.9 13.5 %collective-permute-start.1 = (bf16[196,1536]{1,0:T(8,128)(2,1)}, bf16[196,1536]{1,0:T(8,128)(2,1)}, u32[]{:S(2)}, u32[]{:S(2)}) collective-permute-start(bf16[196,1536]{1,0:T(8,128)(2,1)} %get-tuple-element.158), channel_id=1, source_target_pairs={{0,31},{1,0},{2,1},{3,2},{4,3},{5,4},{6,5},{7,6},{8,7},{9,8},{10,9... | collective-permute-start | bytes 1806344 | tf_op jit(solution)/shard_map/ppermute | solution.py:21
  115.2 2.6 copy-start.2
  117.8 1.6 copy-start.3
  279.3 2.1 copy-start.4
  279.3 2.5 copy-start.5
  294.3 31.1 %collective-permute-start.2 = (bf16[4,196,1536]{2,0,1:T(4,128)(2,1)}, bf16[4,196,1536]{2,0,1:T(4,128)(2,1)S(1)}, u32[]{:S(2)}, u32[]{:S(2)}) collective-permute-start(bf16[4,196,1536]{2,0,1:T(4,128)(2,1)} %copy.52), channel_id=1, source_target_pairs={{0,1},{1,2},{2,3},{3,4},{4,5},{5,6},{6,7},{7,8},{8,9},{9,10},{10,1... | collective-permute-start | bytes 7225352 | tf_op jit(solution)/shard_map/ppermute | solution.py:21
  325.5 1.4 copy-start.1
  336.5 202.8 %reduce-scatter.7.cloned.1.call-start = ((), (), s32[]{:S(2)}) async-start(), calls=%async_computation.4 | async-start | bytes 884736
  471.4 6.3 %copy-start.6 = (bf16[1,196,1536]{1,2,0:T(8,128)(2,1)S(1)}, bf16[1,196,1536]{1,2,0:T(8,128)(2,1)}, u32[]{:S(2)}) copy-start(bf16[1,196,1536]{1,2,0:T(8,128)(2,1)} %copy.62) | copy-start | bytes 1806340
Sparse Core Ops, SparseCore 0:
  10.6 89.6 all-gather.1
  336.6 126.1 reduce-scatter.4
  466.7 72.5 reduce-scatter.6
where the time goes:
time: 551 us; the launch traced here: 547 us
  waiting for transfers between devices  288 us (52%)
  matrix products  166 us (30%)
  local copies, waits for them, and re-layouts  48 us (9%)
  other arithmetic  23 us (4%)
  between operations  13.8 us (3%)
  starting transfers between devices  8.75 us (2%)
    reduce_scatter x1, waiting for transfers between devices, per_device(): lax.psum_scatter(lax.dot_general(attended, cot_in, leading_dims, preferre...  116 us
    all_gather x1, waiting for transfers between devices, per_device(): lax.all_gather(w_out, 'dp', axis=0, tiled=True)  83.5 us
    unnamed x4, waiting for transfers between devices  56.8 us
    dot_general x12, matrix products, window_pass(): jnp.einsum('wgqk,wqge->wkge', probs_low, attn_cot, preferred_element_type...  32.7 us
    dot_general x12, matrix products, window_pass(): jnp.einsum('wgqk,wkge->wqge', probs_low, values, preferred_element_type=j...  32.6 us
    ppermute x3, waiting for transfers between devices, from_behind(): return lax.ppermute(value, axis, pairs)  31.1 us
    dot_general x12, matrix products, window_pass(): jnp.einsum('wgqk,wqge->wkge', grad_scores, queries, preferred_element_typ...  23.1 us
    sub x12, matrix products, window_pass(): exp_scores = jnp.exp(scores - row_max)  22 us
  transfers between devices with their start and end apart: 6, of which 4 were waited for; matrix products, arithmetic and copies ran while one was open for 9% of the time, Pallas kernels for 0%

commit v1 on v0

v1 whole, which is shorter than its diff:
```python
import functools
import math

import jax
import jax.numpy as jnp
from jax import lax
from jax.experimental import pallas as pl
from jax.experimental.pallas import tpu as pltpu
from jax.sharding import PartitionSpec as P

MESH = pl.DeviceIdType.MESH
f32, bf16 = jnp.float32, jnp.bfloat16

HEADS = 24
HEAD_DIM = 64
D = 1536
SPATIAL = 49
WIN_T = 8
FRAMES = 256
TOK = 392
HALF = 196
BLK = 208
LO = 192
QP = 256
PAIRS = HEADS // 2
CHUNK = 512
GROUP = 384
NEG = -1e30
NT = (((1,), (1,)), ((), ()))


def dot(a, b):
    return jnp.dot(a, b, preferred_element_type=f32)


def dot_nt(a, b):
    return lax.dot_general(a, b, NT, preferred_element_type=f32)


def frame_of(row):
    frame = jnp.zeros_like(row)
    for i in range(1, WIN_T):
        frame = frame + jnp.where(row >= SPATIAL * i, 1, 0)
    return frame


def cols(p, width):
    return pl.ds(pl.multiple_of(p * width, 128), width)


def kernel(
    qkv_hbm, w_hbm, dout_hbm, clip_ref,
    mixed_hbm, dqkv_hbm, dw_ref,
    qkv_s, dout_s, kv_win, q_win, dwin, w_all, probs, o_f32, o_rows, att_win,
    cot_win, ds_s, dkv_win, rdkv, dq_win, kaug, qaug,
    g_all, acc, sa1, sb1, sc1, ra1, rb1, rc1, sa2, sb2, sc2, ra2, rb2, rc2,
    fin, zs, zr, fs, fr,
    loc, hs, hr, wxs, wxr, wbs, wbr, ds_sem, dr_sem, os_sem, or_sem,
    gs, gr, r1s, r1r, r2s, r2r, zss, zrs, fss, frs,
):
    dp, tm = lax.axis_index("dp"), lax.axis_index("tm")
    x, yh = dp // 2, dp % 2
    yl, z, core = tm // 16, (tm // 2) % 8, tm % 2
    y = yh * 2 + yl
    step = 1 - 2 * core

    def at(x_, y_, z_, c_):
        return (x_ * 2 + y_ // 2, (y_ % 2) * 16 + z_ * 2 + c_)

    def along_x(d):
        return at((x + d + 4) % 4, y, z, core)

    def along_y(d):
        return at(x, (y + d + 4) % 4, z, core)

    prev, nxt = (dp, (tm + 31) % 32), (dp, (tm + 1) % 32)
    sib = (dp, tm + step)
    y_mate = at(x, 3 - y, z, core)
    final_mate = (dp + 1 - 2 * yh, tm)

    def rcopy(src, dst, ssem, rsem, dev):
        return pltpu.make_async_remote_copy(
            src_ref=src, dst_ref=dst, send_sem=ssem, recv_sem=rsem, device_id=dev, device_id_type=MESH
        )

    loads = [
        pltpu.make_async_copy(qkv_hbm.at[1], qkv_s.at[1], loc.at[1]),
        pltpu.make_async_copy(qkv_hbm.at[2], qkv_s.at[2], loc.at[2]),
        pltpu.make_async_copy(qkv_hbm.at[0], qkv_s.at[0], loc.at[0]),
        pltpu.make_async_copy(dout_hbm, dout_s, loc.at[3]),
        pltpu.make_async_copy(w_hbm, w_all.at[pl.ds(pl.multiple_of(dp * 192, 192), 192)], loc.at[4]),
    ]
    for load in loads:
        load.start()

    barrier = pltpu.get_barrier_semaphore()
    peers = [prev, nxt, along_x(1), along_x(2), along_x(3), along_y(1), along_y(3), final_mate]
    peers += [at(x, y, (z + d) % 8, core) for d in range(1, 8)]
    for dev in peers:
        pl.semaphore_signal(barrier, inc=1, device_id=dev, device_id_type=MESH)
    pl.semaphore_wait(barrier, len(peers))

    def w_rows(src_dp, half):
        return pl.ds(pl.multiple_of(src_dp * 192 + half * 96, 96), 96)

    other = dp + 1 - 2 * yh
    mine = w_hbm.at[pl.ds(pl.multiple_of(core * 96, 96), 96)]

    def w_y():
        return rcopy(mine, w_all.at[w_rows(dp, core)], wxs.at[0], wxr.at[0], y_mate)

    def w_x(d, which):
        i = d if which == 0 else 3 + d
        if which == 0:
            return rcopy(mine, w_all.at[w_rows(dp, core)], wxs.at[i], wxr.at[i], along_x(d))
        rows = w_rows(other, core)
        return rcopy(w_all.at[rows], w_all.at[rows], wxs.at[i], wxr.at[i], along_x(d))

    def w_sib(d, which):
        i = d if which == 0 else 3 + d
        src = ((x + 4 - d) % 4) * 2 + (yh if which == 0 else 1 - yh)
        rows = w_rows(src, core)
        return rcopy(w_all.at[rows], w_all.at[rows], wbs.at[i], wbr.at[i], sib)

    def w_sib_y():
        rows = w_rows(other, core)
        return rcopy(w_all.at[rows], w_all.at[rows], wbs.at[0], wbr.at[0], sib)

    w_y().start()

    loads[0].wait()
    loads[1].wait()
    for t in range(2):
        kv_win[0, t, BLK:, :] = qkv_s[1 + t, 0:BLK, :]
        kv_win[1, t, 0:192, :] = qkv_s[1 + t, LO:384, :]
        kv_win[1, t, 192:200, :] = qkv_s[1 + t, 384:392, :]
        kv_win[1, t, 200:208, :] = jnp.zeros((8, D), bf16)

    def halo(to_next, c):
        if to_next:
            part = kv_win.at[1, :, 0:BLK, c * CHUNK : (c + 1) * CHUNK]
            there = kv_win.at[0, :, 0:BLK, c * CHUNK : (c + 1) * CHUNK]
            return rcopy(part, there, hs.at[0, c], hr.at[0, c], nxt)
        part = kv_win.at[0, :, BLK : 2 * BLK, c * CHUNK : (c + 1) * CHUNK]
        there = kv_win.at[1, :, BLK : 2 * BLK, c * CHUNK : (c + 1) * CHUNK]
        return rcopy(part, there, hs.at[1, c], hr.at[1, c], prev)

    for c in range(3):
        halo(True, c).start()
        halo(False, c).start()
    for d in (1, 3, 2):
        w_x(d, 0).start()

    loads[2].wait()
    q_win[0, 0:BLK, :] = qkv_s[0, 0:BLK, :] * jnp.asarray(0.125, bf16)
    q_win[1, 0:192, :] = qkv_s[0, LO:384, :] * jnp.asarray(0.125, bf16)
    q_win[1, 192:200, :] = qkv_s[0, 384:392, :] * jnp.asarray(0.125, bf16)
    q_win[1, 200:208, :] = jnp.zeros((8, D), bf16)
    q_win[:, BLK:, :] = jnp.zeros((2, QP - BLK, D), bf16)

    loads[3].wait()
    row16 = lax.broadcasted_iota(jnp.int32, (16, D), 0)
    zero16 = jnp.zeros((16, D), f32)
    edge = dout_s[192:208, :].astype(f32)
    dwin[0, 0:192, :] = dout_s[0:192, :]
    dwin[0, 192:208, :] = jnp.where(row16 < HALF - LO, edge, zero16).astype(bf16)
    dwin[0, 208:256, :] = jnp.zeros((48, D), bf16)
    dwin[0, 256:272, :] = jnp.where(row16 >= HALF - LO, edge, zero16).astype(bf16)
    dwin[0, 272:448, :] = dout_s[208:384, :]
    dwin[0, 448:456, :] = dout_s[384:392, :]
    dwin[0, 456:464, :] = jnp.zeros((8, D), bf16)
    dwin[0, 464:512, :] = jnp.zeros((48, D), bf16)
    cot_win[:, BLK:, :] = jnp.zeros((2, QP - BLK, GROUP), bf16)

    def d_copy():
        return rcopy(dwin.at[0], dwin.at[1], ds_sem.at[0], dr_sem.at[0], sib)

    d_copy().start()

    row = lax.broadcasted_iota(jnp.int32, (BLK, 128), 0)
    lane = lax.broadcasted_iota(jnp.int32, (BLK, 128), 1)
    row_q = lax.broadcasted_iota(jnp.int32, (QP, 128), 0)
    lane_q = lax.broadcasted_iota(jnp.int32, (QP, 128), 1)
    for half in range(2):
        clips = [clip_ref[0, (tm * 8 + FRAMES - 4 + 8 * half + w) % FRAMES] for w in range(WIN_T)]
        of_lane = jnp.full((BLK, 128), -1, jnp.int32)
        for w in range(WIN_T):
            of_lane = jnp.where(lane == w, clips[w], of_lane)
        for part in range(2):
            if part == 0:
                frame, real = frame_of(row + LO) - 4, jnp.logical_and(row >= HALF - LO, row < TOK - LO)
            else:
                frame, real = frame_of(row) + 4, row < HALF
            of_row = jnp.full((BLK, 128), -2, jnp.int32)
            for w in range(WIN_T):
                of_row = jnp.where(frame == w, clips[w], of_row)
            seen = jnp.logical_and(real, of_row == of_lane)
            bias = jnp.where(jnp.logical_or(seen, lane >= WIN_T), 0.0, NEG)
            kaug[half, part * BLK : (part + 1) * BLK, :] = bias.astype(bf16)
        if half == 0:
            frame, real = frame_of(row_q) + 4, row_q < HALF
        else:
            frame = frame_of(row_q + LO) - 4
            real = jnp.logical_and(row_q >= HALF - LO, row_q < TOK - LO)
        qaug[half] = jnp.where(jnp.logical_and(real, lane_q == frame), 1.0, 0.0).astype(bf16)

    low = lane_q < HEAD_DIM
    none = jnp.zeros((QP, 128), bf16)
    q_lane = lax.broadcasted_iota(jnp.int32, (1, QP), 1)

    def pick(value, h):
        return jnp.where(low, value, none) if h == 0 else jnp.where(low, none, value)

    def forward(half, p):
        c = cols(p, 128)
        q = q_win[half, :, c]
        keys = jnp.concatenate([kv_win[half, 0, :, c], kaug[half]], axis=1)
        marks = qaug[half]
        for h in range(2):
            s = dot_nt(keys, jnp.concatenate([pick(q, h), marks], axis=1))
            e = jnp.exp(s - jnp.max(s, axis=0, keepdims=True))
            total = jnp.sum(e, axis=0, keepdims=True)
            probs[half, p, h] = (e * (1.0 / total)).astype(bf16)
        start = jnp.where(half == 0, 0, HALF - LO)
        valid = jnp.logical_and(q_lane >= start, q_lane < start + HALF).astype(f32)
        vt = kv_win[half, 1, :, c].T
        outs = []
        for h in range(2):
            outs.append(dot(vt[64 * h : 64 * h + 64], probs[half, p, h]) * valid)
        o = jnp.concatenate(outs, axis=0)
        o_f32[half, pl.ds(pl.multiple_of(p * 128, 128), 128), :] = o
        low_o = o.astype(bf16)
        for j in range(8):
            r = p * 8 + j
            o_rows[r // 6, r % 6, :, cols(half, QP)] = low_o[16 * j : 16 * j + 16]
        att_win[half, :, c] = low_o.T[0:BLK]

    def o_copy(half):
        rows = pl.ds(3 * (1 - core), 3)
        return rcopy(
            o_rows.at[:, rows, :, cols(half, QP)],
            o_rows.at[:, rows, :, pl.ds(pl.multiple_of(512 + half * QP, QP), QP)],
            os_sem.at[half], or_sem.at[half], sib,
        )

    for turn in range(2):
        half = 1 - core if turn == 0 else core
        for c in range(3):
            pltpu.make_async_remote_copy(
                src_ref=kv_win.at[0, :, 0:BLK, 0:CHUNK],
                dst_ref=kv_win.at[half, :, pl.ds(pl.multiple_of(half * BLK, BLK), BLK), c * CHUNK : (c + 1) * CHUNK],
                send_sem=hs.at[0, c], recv_sem=hr.at[half, c], device_id=nxt, device_id_type=MESH,
            ).wait_recv()

            @pl.loop(0, 4)
            def _(i):
                forward(half, c * 4 + i)

        o_copy(half).start()
        if turn == 0:
            w_y().wait_recv()
            w_sib_y().start()
            for d in (1, 3, 2):
                w_x(d, 1).start()

    d_copy().wait_recv()
    o_copy(0).wait_recv()
    o_copy(1).wait_recv()

    @pl.loop(0, 4)
    def _(i):
        lhs = o_rows[:, pl.ds(3 * core, 3), :, :].reshape(768, 1024)
        rhs = dwin[:, :, cols(i, GROUP)].reshape(1024, GROUP)
        g_all[i] = dot(lhs, rhs)

    def ring_dev(axis, d):
        return along_y(d) if axis == 0 else along_x(d)

    def ring_at(axis, d):
        if axis == 0:
            to = (y + 4 + d * step) % 4
            return (to % 2) * 2 + to // 2
        return (x + 4 + d * step) % 4

    def piece1(inst, d):
        where = ring_at(inst, d)
        if inst == 0:
            return g_all[:, pl.ds(pl.multiple_of(where * 192, 96), 96), :]
        return jnp.stack([g_all[where, r * 192 + 96 : r * 192 + 192, :] for r in range(4)])

    def send1(inst, kind):
        src, dst = ((sa1, ra1), (sb1, rb1), (sc1, rc1))[kind]
        dev = ring_dev(inst, step if kind < 2 else -step)
        return rcopy(src.at[inst], dst.at[inst], r1s.at[inst, kind], r1r.at[inst, kind], dev)

    def send2(inst, kind):
        src, dst = ((sa2, ra2), (sb2, rb2), (sc2, rc2))[kind]
        dev = ring_dev(1 - inst, step if kind < 2 else -step)
        return rcopy(src.at[inst], dst.at[inst], r2s.at[inst, kind], r2r.at[inst, kind], dev)

    def sum1_start():
        for inst in range(2):
            sa1[inst] = piece1(inst, 2).astype(bf16)
            send1(inst, 0).start()
            sc1[inst] = piece1(inst, -1).astype(bf16)
            send1(inst, 2).start()

    def sum1_mid():
        for inst in range(2):
            send1(inst, 0).wait_recv()
            sb1[inst] = (piece1(inst, 1) + ra1[inst].astype(f32)).astype(bf16)
            send1(inst, 1).start()

    def sum2_start():
        for inst in range(2):
            send1(inst, 1).wait_recv()
            send1(inst, 2).wait_recv()
            acc[inst] = piece1(inst, 0) + rb1[inst].astype(f32) + rc1[inst].astype(f32)
            sa2[inst] = acc[inst, ring_at(1 - inst, 2)].astype(bf16)
            send2(inst, 0).start()
            sc2[inst] = acc[inst, ring_at(1 - inst, -1)].astype(bf16)
            send2(inst, 2).start()

    def sum2_mid():
        for inst in range(2):
            send2(inst, 0).wait_recv()
            sb2[inst] = (acc[inst, ring_at(1 - inst, 1)] + ra2[inst].astype(f32)).astype(bf16)
            send2(inst, 1).start()

    def z_copy(j):
        to = yh * 4 + j
        slot = (to + 8 - z) % 8
        return to, rcopy(zs.at[j], zr.at[slot], zss.at[j], zrs.at[slot], at(x, y, to, core))

    def sum3_start():
        for inst in range(2):
            send2(inst, 1).wait_recv()
            send2(inst, 2).wait_recv()
            done = acc[inst, ring_at(1 - inst, 0)] + rb2[inst].astype(f32) + rc2[inst].astype(f32)
            for jj in range(2):
                j = inst * 2 + jj
                fin[j] = done[jj * 48 : jj * 48 + 48]
                zs[j] = done[jj * 48 : jj * 48 + 48].astype(bf16)
                to, copy = z_copy(j)
                pl.when(to != z)(copy.start)

    norm = 1.0 / math.sqrt(8 * 32 * TOK)
    keeper = z // 4 == yh

    def f_copy():
        return rcopy(fs, fr, fss.at[0], frs.at[0], final_mate)

    def sum_end():
        @pl.when(keeper)
        def _():
            total = fin[z % 4]
            for d in range(1, 8):
                rcopy(zs.at[0], zr.at[d], zss.at[0], zrs.at[d], sib).wait_recv()
                total = total + zr[d].astype(f32)
            total = total * norm
            left, right = total[:, 0:192], total[:, 192:384]
            dw_ref[...] = jnp.where(yh == 0, left, right)
            fs[...] = jnp.where(yh == 0, right, left)
            f_copy().start()

    def sum_last():
        @pl.when(jnp.logical_not(keeper))
        def _():
            f_copy().wait_recv()
            dw_ref[...] = fr[...]

    sum1_start()

    loads[4].wait()
    order = (0, 1, 3, 2)

    def backward(half, p, i):
        c = cols(p, 128)
        do = cot_win[half, :, cols(i, 128)]
        keys, values = kv_win[half, 0, :, c], kv_win[half, 1, :, c]
        q = q_win[half, :, c]
        prod = do.T.astype(f32) * o_f32[half, pl.ds(pl.multiple_of(p * 128, 128), 128), :]
        for h in range(2):
            grad = dot_nt(values, pick(do, h))
            total = jnp.sum(prod[64 * h : 64 * h + 64], axis=0, keepdims=True)
            ds_s[half, h] = (probs[half, p, h].astype(f32) * (grad - total)).astype(bf16)
        kt = keys.T
        dq = jnp.concatenate([dot(kt[64 * h : 64 * h + 64], ds_s[half, h]) for h in range(2)], axis=0) * 0.125
        dq_win[half, :, c] = dq.astype(bf16).T[0:BLK]
        dkv_win[half, 1, :, c] = (dot(probs[half, p, 0], pick(do, 0)) + dot(probs[half, p, 1], pick(do, 1))).astype(bf16)
        dkv_win[half, 0, :, c] = (dot(ds_s[half, 0], pick(q, 0)) + dot(ds_s[half, 1], pick(q, 1))).astype(bf16)

    def g_copy(to_next, k):
        c = cols((x + 4 - order[k]) % 4, GROUP)
        if to_next:
            return rcopy(dkv_win.at[1, :, BLK : 2 * BLK, c], rdkv.at[0, :, :, c], gs.at[0, k], gr.at[0, k], nxt)
        return rcopy(dkv_win.at[0, :, 0:BLK, c], rdkv.at[1, :, :, c], gs.at[1, k], gr.at[1, k], prev)

    def pass_on(d):
        for which in range(2):
            w_x(d, which).wait_recv()
            w_sib(d, which).start()

    w_sib_y().wait_recv()
    for k, d in enumerate(order):
        g = (x + 4 - d) % 4
        if d:
            for which in range(2):
                w_sib(d, which).wait_recv()
        for half in range(2):
            cot_win[half, 0:BLK, :] = dot_nt(
                dwin[0, half * QP : half * QP + BLK, :], w_all[pl.ds(pl.multiple_of(g * GROUP, GROUP), GROUP), :]
            ).astype(bf16)
        if k + 1 < 4:
            pass_on(order[k + 1])

        @pl.loop(0, 3)
        def _(i):
            for half in range(2):
                backward(half, g * 3 + i, i)

        g_copy(True, k).start()
        g_copy(False, k).start()
        (sum1_mid, sum2_start, sum2_mid, sum3_start)[k]()

    @pl.loop(0, 3)
    def _(i):
        c = cols(i, 512)
        w = w_all[:, c]
        first = dot(att_win[0], w)
        second = dot(att_win[1], w)
        dout_s[0:192, c] = first[0:192].astype(bf16)
        dout_s[192:208, c] = (first[192:208] + second[0:16]).astype(bf16)
        dout_s[208:392, c] = second[16:200].astype(bf16)

    out_mixed = pltpu.make_async_copy(dout_s, mixed_hbm, loc.at[5])
    out_mixed.start()
    qkv_s[0, 0:192, :] = dq_win[0, 0:192, :]
    qkv_s[0, 192:208, :] = dq_win[0, 192:208, :] + dq_win[1, 0:16, :]
    qkv_s[0, 208:392, :] = dq_win[1, 16:200, :]
    out_q = pltpu.make_async_copy(qkv_s.at[0], dqkv_hbm.at[0], loc.at[6])
    out_q.start()
    sum_end()
    for k in range(4):
        g_copy(True, k).wait_recv()
        g_copy(False, k).wait_recv()
    outs = []
    for t in range(2):
        first = dkv_win[0, t, BLK:, :].astype(f32) + rdkv[0, t].astype(f32)
        second = dkv_win[1, t, 0:BLK, :].astype(f32) + rdkv[1, t].astype(f32)
        qkv_s[1 + t, 0:192, :] = first[0:192].astype(bf16)
        qkv_s[1 + t, 192:208, :] = (first[192:208] + second[0:16]).astype(bf16)
        qkv_s[1 + t, 208:392, :] = second[16:200].astype(bf16)
        outs.append(pltpu.make_async_copy(qkv_s.at[1 + t], dqkv_hbm.at[1 + t], loc.at[7 + t]))
        outs[t].start()
    sum_last()

    w_y().wait_send()
    w_sib_y().wait_send()
    for d in (1, 2, 3):
        for which in range(2):
            w_x(d, which).wait_send()
            w_sib(d, which).wait_send()
    for c in range(3):
        halo(True, c).wait_send()
        halo(False, c).wait_send()
    d_copy().wait_send()
    for half in range(2):
        o_copy(half).wait_send()
    for k in range(4):
        g_copy(True, k).wait_send()
        g_copy(False, k).wait_send()
    for inst in range(2):
        for kind in range(3):
            send1(inst, kind).wait_send()
            send2(inst, kind).wait_send()
    for j in range(4):
        to, copy = z_copy(j)
        pl.when(to != z)(copy.wait_send)
    pl.when(keeper)(lambda: f_copy().wait_send())
    out_mixed.wait()
    out_q.wait()
    for out in outs:
        out.wait()


def per_device(qkv, w_out, d_out, clip_ids):
    hbm = pl.BlockSpec(memory_space=pl.ANY)
    vmem = pltpu.VMEM
    dma = pltpu.SemaphoreType.DMA
    mixed, grads, d_weight = pl.pallas_call(
        kernel,
        in_specs=[hbm, hbm, hbm, pl.BlockSpec(memory_space=pltpu.SMEM)],
        out_specs=[hbm, hbm, pl.BlockSpec(memory_space=pltpu.VMEM)],
        out_shape=[
            jax.ShapeDtypeStruct((TOK, D), bf16),
            jax.ShapeDtypeStruct((3, TOK, D), bf16),
            jax.ShapeDtypeStruct((48, 192), f32),
        ],
        scratch_shapes=[
            vmem((3, TOK, D), bf16),
            vmem((TOK, D), bf16),
            vmem((2, 2, 2 * BLK, D), bf16),
            vmem((2, QP, D), bf16),
            vmem((2, 2 * QP, D), bf16),
            vmem((D, D), bf16),
            vmem((2, PAIRS, 2, 2 * BLK, QP), bf16),
            vmem((2, D, QP), f32),
            vmem((16, 6, 16, 4 * QP), bf16),
            vmem((2, BLK, D), bf16),
            vmem((2, QP, GROUP), bf16),
            vmem((2, 2, 2 * BLK, QP), bf16),
            vmem((2, 2, 2 * BLK, D), bf16),
            vmem((2, 2, BLK, D), bf16),
            vmem((2, BLK, D), bf16),
            vmem((2, 2 * BLK, 128), bf16),
            vmem((2, QP, 128), bf16),
            vmem((4, 768, GROUP), f32),
            vmem((2, 4, 96, GROUP), f32),
        ]
        + [vmem((2, 4, 96, GROUP), bf16)] * 6
        + [vmem((2, 96, GROUP), bf16)] * 6
        + [
            vmem((4, 48, GROUP), f32),
            vmem((4, 48, GROUP), bf16),
            vmem((8, 48, GROUP), bf16),
            vmem((48, 192), f32),
            vmem((48, 192), f32),
            dma((9,)),
            dma((2, 3)), dma((2, 3)),
            dma((7,)), dma((7,)), dma((7,)), dma((7,)),
            dma((1,)), dma((1,)), dma((2,)), dma((2,)),
            dma((2, 4)), dma((2, 4)),
            dma((2, 3)), dma((2, 3)), dma((2, 3)), dma((2, 3)),
            dma((4,)), dma((8,)), dma((1,)), dma((1,)),
        ],
        compiler_params=pltpu.CompilerParams(
            collective_id=0, has_side_effects=True, vmem_limit_bytes=62 << 20
        ),
    )(qkv[0], w_out, d_out[0], clip_ids)
    return mixed[None], grads[None], d_weight


def solution(mesh):
    return jax.shard_map(
        per_device,
        mesh=mesh,
        in_specs=(P("dp", None, "tm", None), P("dp", None), P("dp", "tm", None), P("dp", None)),
        out_specs=(P("dp", "tm", None), P("dp", None, "tm", None), P("tm", "dp")),
        check_vma=False,
    )
```

time: 551 us -> 83.9 us (0.15)
  the two profiles are of different devices: /device:TPU:10 before, /device:TPU:168 now
where the time goes in v1:
time: 83.9 us; the launch traced here: 83.8 us
  Pallas kernels  76 us (91%)
  local copies, waits for them, and re-layouts  7.14 us (9%)
    pallas_call x1, Pallas kernels, per_device(): pl.pallas_call(kernel, in_specs=[hbm, hbm, hbm, pl.BlockSpec(memory_space...  76 us
    unnamed x5, local copies, waits for them, and re-layouts  7.14 us

profile of v1, /device:TPU:168, one launch (start us, length us, event | category | flops | bytes accessed | tf_op | source)
XLA Modules:
  0.0 83.8 jit_solution(11908493520063622635)
XLA Ops:
  0.6 76.0 %shard_map.67 = (bf16[392,1536]{1,0:T(8,128)(2,1)}, bf16[3,392,1536]{2,1,0:T(8,128)(2,1)}, f32[48,192]{1,0:T(8,128)}) custom-call(bf16[3,392,1536]{2,1,0:T(8,128)(2,1)} %bitcast.4, bf16[192,1536]{1,0:T(8,128)(2,1)} %w_hbm.1, bf16[392,1536]{1,0:T(8,128)(2,1)} %bitcast.7, s32[1,256]{1,0:T(1,128)} %clip_ref.1), custom_call_target="tpu_custom_call" | custom-call | tf_op jit(solution)/shard_map/pallas_call | solution.py:491
  76.6 2.4 %copy.10 = bf16[1,392,1536]{2,1,0:T(8,128)(2,1)} copy(bf16[1,392,1536]{2,1,0:T(8,128)(2,1)} %bitcast.6) | data formatting | bytes 2408448
  79.0 0.0 copy-start
  79.0 4.1 %copy.11 = bf16[1,3,392,1536]{3,2,1,0:T(8,128)(2,1)} copy(bf16[1,3,392,1536]{3,2,1,0:T(8,128)(2,1)} %bitcast.5) | data formatting | bytes 7225344
  83.2 0.0 copy-done
  83.2 0.6 copy.12
Async XLA Ops:
  79.0 4.1 %copy-start = (f32[48,192]{1,0:T(8,128)S(1)}, f32[48,192]{1,0:T(8,128)}, u32[]{:S(2)}) copy-start(f32[48,192]{1,0:T(8,128)} %get-tuple-element.14) | copy-start | bytes 110596

commit v2 on v1

--- a/solution.py
+++ b/solution.py
@@ -23,7 +23,9 @@
 LO = 192
 QP = 256
 PAIRS = HEADS // 2
-CHUNK = 512
+CHUNK = 256
+STEPS = D // CHUNK
+PER = CHUNK // 128
 GROUP = 384
 NEG = -1e30
 NT = (((1,), (1,)), ((), ()))
@@ -55,7 +57,7 @@
     cot_win, ds_s, dkv_win, rdkv, dq_win, kaug, qaug,
     g_all, acc, sa1, sb1, sc1, ra1, rb1, rc1, sa2, sb2, sc2, ra2, rb2, rc2,
     fin, zs, zr, fs, fr,
-    loc, hs, hr, wxs, wxr, wbs, wbr, ds_sem, dr_sem, os_sem, or_sem,
+    loc, hs, hr, ws, wr, wbs, wbr, ds_sem, dr_sem, os_sem, or_sem,
     gs, gr, r1s, r1r, r2s, r2r, zss, zrs, fss, frs,
 ):
     dp, tm = lax.axis_index("dp"), lax.axis_index("tm")
@@ -75,8 +77,9 @@
 
     prev, nxt = (dp, (tm + 31) % 32), (dp, (tm + 1) % 32)
     sib = (dp, tm + step)
-    y_mate = at(x, 3 - y, z, core)
     final_mate = (dp + 1 - 2 * yh, tm)
+
+    across = at(x, 3 - y, z, core)
 
     def rcopy(src, dst, ssem, rsem, dev):
         return pltpu.make_async_remote_copy(
@@ -88,45 +91,41 @@
         pltpu.make_async_copy(qkv_hbm.at[2], qkv_s.at[2], loc.at[2]),
         pltpu.make_async_copy(qkv_hbm.at[0], qkv_s.at[0], loc.at[0]),
         pltpu.make_async_copy(dout_hbm, dout_s, loc.at[3]),
-        pltpu.make_async_copy(w_hbm, w_all.at[pl.ds(pl.multiple_of(dp * 192, 192), 192)], loc.at[4]),
+        pltpu.make_async_copy(
+            w_hbm, w_all.at[pl.ds(pl.multiple_of(dp * 192, 192), 192)], loc.at[4]
+        ),
     ]
     for load in loads:
         load.start()
 
     barrier = pltpu.get_barrier_semaphore()
-    peers = [prev, nxt, along_x(1), along_x(2), along_x(3), along_y(1), along_y(3), final_mate]
+    peers = [prev, nxt, along_x(1), along_x(2), along_x(3), along_y(1), along_y(2), along_y(3)]
     peers += [at(x, y, (z + d) % 8, core) for d in range(1, 8)]
     for dev in peers:
         pl.semaphore_signal(barrier, inc=1, device_id=dev, device_id_type=MESH)
-    pl.semaphore_wait(barrier, len(peers))
-
-    def w_rows(src_dp, half):
-        return pl.ds(pl.multiple_of(src_dp * 192 + half * 96, 96), 96)
-
-    other = dp + 1 - 2 * yh
-    mine = w_hbm.at[pl.ds(pl.multiple_of(core * 96, 96), 96)]
-
-    def w_y():
-        return rcopy(mine, w_all.at[w_rows(dp, core)], wxs.at[0], wxr.at[0], y_mate)
-
-    def w_x(d, which):
-        i = d if which == 0 else 3 + d
-        if which == 0:
-            return rcopy(mine, w_all.at[w_rows(dp, core)], wxs.at[i], wxr.at[i], along_x(d))
-        rows = w_rows(other, core)
-        return rcopy(w_all.at[rows], w_all.at[rows], wxs.at[i], wxr.at[i], along_x(d))
+
+    def w_rows(d, which):
+        src = ((x + 4 - d) % 4) * 2 + (yh if which == 0 else 1 - yh)
+        return w_all.at[pl.ds(pl.multiple_of(src * 192 + core * 96, 96), 96)]
+
+    def w_copy(d, which):
+        if (d, which) == (0, 1):
+            rows, dev = w_rows(0, 0), across
+        elif (d, which) == (2, 1):
+            rows, dev = w_rows(2, 0), across
+        else:
+            rows, dev = w_rows(0, which), along_x(d)
+        return rcopy(rows, rows, ws.at[d, which], wr.at[d, which], dev)
 
     def w_sib(d, which):
-        i = d if which == 0 else 3 + d
-        src = ((x + 4 - d) % 4) * 2 + (yh if which == 0 else 1 - yh)
-        rows = w_rows(src, core)
-        return rcopy(w_all.at[rows], w_all.at[rows], wbs.at[i], wbr.at[i], sib)
-
-    def w_sib_y():
-        rows = w_rows(other, core)
-        return rcopy(w_all.at[rows], w_all.at[rows], wbs.at[0], wbr.at[0], sib)
-
-    w_y().start()
+        rows = w_rows(d, which)
+        return rcopy(rows, rows, wbs.at[d, which], wbr.at[d, which], sib)
+
+    def w_arrived(d, which):
+        w_copy(d, which).wait_recv()
+        w_sib(d, which).start()
+
+    pieces = [(0, 1)] + [(d, which) for d in (1, 3, 2) for which in range(2)]
 
     loads[0].wait()
     loads[1].wait()
@@ -145,11 +144,13 @@
         there = kv_win.at[1, :, BLK : 2 * BLK, c * CHUNK : (c + 1) * CHUNK]
         return rcopy(part, there, hs.at[1, c], hr.at[1, c], prev)
 
-    for c in range(3):
+    pl.semaphore_wait(barrier, len(peers))
+    for c in range(STEPS):
         halo(True, c).start()
         halo(False, c).start()
-    for d in (1, 3, 2):
-        w_x(d, 0).start()
+    loads[4].wait()
+    for piece in ((0, 1), (1, 0), (3, 0), (2, 0)):
+        w_copy(*piece).start()
 
     loads[2].wait()
     q_win[0, 0:BLK, :] = qkv_s[0, 0:BLK, :] * jnp.asarray(0.125, bf16)
@@ -211,7 +212,7 @@
     def pick(value, h):
         return jnp.where(low, value, none) if h == 0 else jnp.where(low, none, value)
 
-    def forward(half, p):
+    def softmax(half, p):
         c = cols(p, 128)
         q = q_win[half, :, c]
         keys = jnp.concatenate([kv_win[half, 0, :, c], kaug[half]], axis=1)
@@ -221,6 +222,9 @@
             e = jnp.exp(s - jnp.max(s, axis=0, keepdims=True))
             total = jnp.sum(e, axis=0, keepdims=True)
             probs[half, p, h] = (e * (1.0 / total)).astype(bf16)
+
+    def attend(half, p):
+        c = cols(p, 128)
         start = jnp.where(half == 0, 0, HALF - LO)
         valid = jnp.logical_and(q_lane >= start, q_lane < start + HALF).astype(f32)
         vt = kv_win[half, 1, :, c].T
@@ -243,35 +247,58 @@
             os_sem.at[half], or_sem.at[half], sib,
         )
 
+    def weight_grad(turn):
+        own, there = (1 - core, core) if turn == 0 else (core, 1 - core)
+        o_copy(there).wait_recv()
+
+        @pl.loop(0, 4)
+        def _(i):
+            sub = pl.ds(3 * core, 3)
+            lhs = jnp.concatenate(
+                [
+                    o_rows[:, sub, :, cols(own, QP)].reshape(768, QP),
+                    o_rows[:, sub, :, pl.ds(pl.multiple_of(512 + there * QP, QP), QP)].reshape(768, QP),
+                ],
+                axis=1,
+            )
+            rhs = jnp.concatenate(
+                [
+                    dwin[0, pl.ds(pl.multiple_of(own * QP, QP), QP), cols(i, GROUP)],
+                    dwin[1, pl.ds(pl.multiple_of(there * QP, QP), QP), cols(i, GROUP)],
+                ],
+                axis=0,
+            )
+            if turn == 0:
+                g_all[i] = dot(lhs, rhs)
+            else:
+                g_all[i] += dot(lhs, rhs)
+
     for turn in range(2):
         half = 1 - core if turn == 0 else core
-        for c in range(3):
+        for c in range(STEPS):
             pltpu.make_async_remote_copy(
                 src_ref=kv_win.at[0, :, 0:BLK, 0:CHUNK],
                 dst_ref=kv_win.at[half, :, pl.ds(pl.multiple_of(half * BLK, BLK), BLK), c * CHUNK : (c + 1) * CHUNK],
                 send_sem=hs.at[0, c], recv_sem=hr.at[half, c], device_id=nxt, device_id_type=MESH,
             ).wait_recv()
 
-            @pl.loop(0, 4)
-            def _(i):
-                forward(half, c * 4 + i)
-
+            for p in range(c * PER, (c + 1) * PER):
+                if c:
+                    attend(half, p - PER)
+            for p in range(c * PER, (c + 1) * PER):
+                softmax(half, p)
+            if c == STEPS - 1:
+                for p in range(c * PER, (c + 1) * PER):
+                    attend(half, p)
+
+            if turn == 0 and c == 5:
+                w_arrived(0, 1)
+                w_copy(1, 1).start()
+                w_copy(3, 1).start()
+            if turn == 1 and c == 1:
+                d_copy().wait_recv()
+                weight_grad(0)
         o_copy(half).start()
-        if turn == 0:
-            w_y().wait_recv()
-            w_sib_y().start()
-            for d in (1, 3, 2):
-                w_x(d, 1).start()
-
-    d_copy().wait_recv()
-    o_copy(0).wait_recv()
-    o_copy(1).wait_recv()
-
-    @pl.loop(0, 4)
-    def _(i):
-        lhs = o_rows[:, pl.ds(3 * core, 3), :, :].reshape(768, 1024)
-        rhs = dwin[:, :, cols(i, GROUP)].reshape(1024, GROUP)
-        g_all[i] = dot(lhs, rhs)
 
     def ring_dev(axis, d):
         return along_y(d) if axis == 0 else along_x(d)
@@ -302,6 +329,9 @@
         for inst in range(2):
             sa1[inst] = piece1(inst, 2).astype(bf16)
             send1(inst, 0).start()
+
+    def sum1_more():
+        for inst in range(2):
             sc1[inst] = piece1(inst, -1).astype(bf16)
             send1(inst, 2).start()
 
@@ -368,11 +398,6 @@
         def _():
             f_copy().wait_recv()
             dw_ref[...] = fr[...]
-
-    sum1_start()
-
-    loads[4].wait()
-    order = (0, 1, 3, 2)
 
     def backward(half, p, i):
         c = cols(p, 128)
@@ -390,38 +415,61 @@
         dkv_win[half, 1, :, c] = (dot(probs[half, p, 0], pick(do, 0)) + dot(probs[half, p, 1], pick(do, 1))).astype(bf16)
         dkv_win[half, 0, :, c] = (dot(ds_s[half, 0], pick(q, 0)) + dot(ds_s[half, 1], pick(q, 1))).astype(bf16)
 
-    def g_copy(to_next, k):
-        c = cols((x + 4 - order[k]) % 4, GROUP)
+    order = (0, 1, 3, 2)
+
+    def w_poll(*which):
+        def poll():
+            for piece in which:
+                w_arrived(*piece)
+            if (2, 0) in which:
+                w_copy(2, 1).start()
+
+        return poll
+
+    polls = {
+        (0, 0): [sum1_more, w_poll((1, 0), (1, 1))],
+        (0, 2): [sum1_mid, w_poll((3, 0), (3, 1))],
+        (1, 0): [w_poll((2, 0))],
+        (1, 2): [sum2_start],
+        (2, 0): [w_poll((2, 1))],
+        (2, 2): [sum2_mid],
+        (3, 1): [sum3_start],
+    }
+
+    def g_copy(to_next, k, part):
+        first, width = ((0, 256), (256, 128))[part]
+        c = pl.ds(pl.multiple_of(((x + 4 - order[k]) % 4) * GROUP + first, 128), width)
+        i = 2 * k + part
         if to_next:
-            return rcopy(dkv_win.at[1, :, BLK : 2 * BLK, c], rdkv.at[0, :, :, c], gs.at[0, k], gr.at[0, k], nxt)
-        return rcopy(dkv_win.at[0, :, 0:BLK, c], rdkv.at[1, :, :, c], gs.at[1, k], gr.at[1, k], prev)
-
-    def pass_on(d):
+            return rcopy(dkv_win.at[1, :, BLK : 2 * BLK, c], rdkv.at[0, :, :, c], gs.at[0, i], gr.at[0, i], nxt)
+        return rcopy(dkv_win.at[0, :, 0:BLK, c], rdkv.at[1, :, :, c], gs.at[1, i], gr.at[1, i], prev)
+
+    def cotangent(k):
+        d = order[k]
         for which in range(2):
-            w_x(d, which).wait_recv()
-            w_sib(d, which).start()
-
-    w_sib_y().wait_recv()
+            if d or which:
+                w_sib(d, which).wait_recv()
+        group = (x + 4 - d) % 4
+        both = jnp.concatenate([dwin[0, 0:BLK, :], dwin[0, QP : QP + BLK, :]], axis=0)
+        cot = dot_nt(both, w_all[pl.ds(pl.multiple_of(group * GROUP, GROUP), GROUP), :]).astype(bf16)
+        cot_win[0, 0:BLK, :] = cot[0:BLK]
+        cot_win[1, 0:BLK, :] = cot[BLK:]
+
+    cotangent(0)
+    weight_grad(1)
+    sum1_start()
     for k, d in enumerate(order):
-        g = (x + 4 - d) % 4
-        if d:
-            for which in range(2):
-                w_sib(d, which).wait_recv()
-        for half in range(2):
-            cot_win[half, 0:BLK, :] = dot_nt(
-                dwin[0, half * QP : half * QP + BLK, :], w_all[pl.ds(pl.multiple_of(g * GROUP, GROUP), GROUP), :]
-            ).astype(bf16)
-        if k + 1 < 4:
-            pass_on(order[k + 1])
-
-        @pl.loop(0, 3)
-        def _(i):
+        if k:
+            cotangent(k)
+        for part in range(3):
             for half in range(2):
-                backward(half, g * 3 + i, i)
-
-        g_copy(True, k).start()
-        g_copy(False, k).start()
-        (sum1_mid, sum2_start, sum2_mid, sum3_start)[k]()
+                backward(half, ((x + 4 - d) % 4) * 3 + part, part)
+            if part:
+                g_copy(True, k, part - 1).start()
+                g_copy(False, k, part - 1).start()
+            if (k, part) in polls:
+                for poll in polls[k, part]:
+                    poll()
 
     @pl.loop(0, 3)
     def _(i):
@@ -442,8 +490,9 @@
     out_q.start()
     sum_end()
     for k in range(4):
-        g_copy(True, k).wait_recv()
-        g_copy(False, k).wait_recv()
+        for part in range(2):
+            g_copy(True, k, part).wait_recv()
+            g_copy(False, k, part).wait_recv()
     outs = []
     for t in range(2):
         first = dkv_win[0, t, BLK:, :].astype(f32) + rdkv[0, t].astype(f32)
@@ -455,21 +504,19 @@
         outs[t].start()
     sum_last()
 
-    w_y().wait_send()
-    w_sib_y().wait_send()
-    for d in (1, 2, 3):
-        for which in range(2):
-            w_x(d, which).wait_send()
-            w_sib(d, which).wait_send()
-    for c in range(3):
+    for piece in pieces:
+        w_copy(*piece).wait_send()
+        w_sib(*piece).wait_send()
+    for c in range(STEPS):
         halo(True, c).wait_send()
         halo(False, c).wait_send()
     d_copy().wait_send()
     for half in range(2):
         o_copy(half).wait_send()
     for k in range(4):
-        g_copy(True, k).wait_send()
-        g_copy(False, k).wait_send()
+        for part in range(2):
+            g_copy(True, k, part).wait_send()
+            g_copy(False, k, part).wait_send()
     for inst in range(2):
         for kind in range(3):
             send1(inst, kind).wait_send()
@@ -480,6 +527,23 @@
     pl.when(keeper)(lambda: f_copy().wait_send())
     out_mixed.wait()
     out_q.wait()
+    for out in outs:
+        out.wait()
+
+
+def settle(mixed_in, grads_in, weight_in, mixed_out, grads_out, weight_out, hold, hold_w, sems):
+    ins = [pltpu.make_async_copy(mixed_in, hold.at[0], sems.at[0, 0])]
+    outs = [pltpu.make_async_copy(hold.at[0], mixed_out, sems.at[1, 0])]
+    for t in range(3):
+        ins.append(pltpu.make_async_copy(grads_in.at[t], hold.at[1 + t], sems.at[0, 1 + t]))
+        outs.append(pltpu.make_async_copy(hold.at[1 + t], grads_out.at[t], sems.at[1, 1 + t]))
+    ins.append(pltpu.make_async_copy(weight_in, hold_w, sems.at[0, 4]))
+    outs.append(pltpu.make_async_copy(hold_w, weight_out, sems.at[1, 4]))
+    for copy in ins:
+        copy.start()
+    for copy, out in zip(ins, outs):
+        copy.wait()
+        out.start()
     for out in outs:
         out.wait()
 
@@ -527,10 +591,10 @@
             vmem((48, 192), f32),
             vmem((48, 192), f32),
             dma((9,)),
-            dma((2, 3)), dma((2, 3)),
-            dma((7,)), dma((7,)), dma((7,)), dma((7,)),
+            dma((2, STEPS)), dma((2, STEPS)),
+            dma((4, 2)), dma((4, 2)), dma((4, 2)), dma((4, 2)),
             dma((1,)), dma((1,)), dma((2,)), dma((2,)),
-            dma((2, 4)), dma((2, 4)),
+            dma((2, 8)), dma((2, 8)),
             dma((2, 3)), dma((2, 3)), dma((2, 3)), dma((2, 3)),
             dma((4,)), dma((8,)), dma((1,)), dma((1,)),
         ],
@@ -538,6 +602,18 @@
             collective_id=0, has_side_effects=True, vmem_limit_bytes=62 << 20
         ),
     )(qkv[0], w_out, d_out[0], clip_ids)
+    mixed, grads, d_weight = pl.pallas_call(
+        settle,
+        in_specs=[hbm] * 3,
+        out_specs=[hbm] * 3,
+        out_shape=[
+            jax.ShapeDtypeStruct((TOK, D), bf16),
+            jax.ShapeDtypeStruct((3, TOK, D), bf16),
+            jax.ShapeDtypeStruct((48, 192), f32),
+        ],
+        scratch_shapes=[vmem((4, TOK, D), bf16), vmem((48, 192), f32), dma((2, 5))],
+        compiler_params=pltpu.CompilerParams(vmem_limit_bytes=62 << 20),
+    )(mixed, grads, d_weight)
     return mixed[None], grads[None], d_weight
 
 

time: 83.9 us -> 79.2 us (0.944)
  the two profiles are of different devices: /device:TPU:168 before, /device:TPU:10 now
where the time goes in v2:
time: 79.2 us; the launch traced here: 79.1 us
  Pallas kernels  78.3 us (99%)
  between operations  0.82 us (1%)
    pallas_call x1, Pallas kernels, per_device(): pl.pallas_call(kernel, in_specs=[hbm, hbm, hbm, pl.BlockSpec(memory_space...  74.4 us
    pallas_call x1, Pallas kernels, per_device(): pl.pallas_call(settle, in_specs=[hbm] * 3, out_specs=[hbm] * 3, out_shape...  3.86 us

profile of v2, /device:TPU:10, one launch (start us, length us, event | category | flops | bytes accessed | tf_op | source)
XLA Modules:
  0.0 79.1 jit_solution(13118402510873538981)
XLA Ops:
  0.6 74.4 %shard_map.67 = (bf16[392,1536]{1,0:T(8,128)(2,1)}, bf16[3,392,1536]{2,1,0:T(8,128)(2,1)}, f32[48,192]{1,0:T(8,128)}) custom-call(bf16[3,392,1536]{2,1,0:T(8,128)(2,1)} %bitcast.4, bf16[192,1536]{1,0:T(8,128)(2,1)} %w_hbm.1, bf16[392,1536]{1,0:T(8,128)(2,1)} %bitcast.5, s32[1,256]{1,0:T(1,128)} %clip_ref.1), custom_call_target="tpu_custom_call" | custom-call | tf_op jit(solution)/shard_map/pallas_call | solution.py:555
  75.1 3.9 %shard_map.68 = (bf16[392,1536]{1,0:T(8,128)(2,1)}, bf16[3,392,1536]{2,1,0:T(8,128)(2,1)}, f32[48,192]{1,0:T(8,128)}) custom-call(bf16[392,1536]{1,0:T(8,128)(2,1)} %get-tuple-element.9.mixed_in, bf16[3,392,1536]{2,1,0:T(8,128)(2,1)} %get-tuple-element.10.grads_in, f32[48,192]{1,0:T(8,128)} %get-tuple-element.11.weight_in), custom_call_target="tpu_custom_call" | custom-call | tf_op jit(solution)/shard_map/pallas_call | solution.py:605

commit v3 on v2

--- a/solution.py
+++ b/solution.py
@@ -330,7 +330,6 @@
             sa1[inst] = piece1(inst, 2).astype(bf16)
             send1(inst, 0).start()
 
-    def sum1_more():
         for inst in range(2):
             sc1[inst] = piece1(inst, -1).astype(bf16)
             send1(inst, 2).start()
@@ -399,21 +398,28 @@
             f_copy().wait_recv()
             dw_ref[...] = fr[...]
 
-    def backward(half, p, i):
+    def score_grad(half, p, i):
         c = cols(p, 128)
         do = cot_win[half, :, cols(i, 128)]
-        keys, values = kv_win[half, 0, :, c], kv_win[half, 1, :, c]
-        q = q_win[half, :, c]
+        values = kv_win[half, 1, :, c]
         prod = do.T.astype(f32) * o_f32[half, pl.ds(pl.multiple_of(p * 128, 128), 128), :]
         for h in range(2):
             grad = dot_nt(values, pick(do, h))
             total = jnp.sum(prod[64 * h : 64 * h + 64], axis=0, keepdims=True)
             ds_s[half, h] = (probs[half, p, h].astype(f32) * (grad - total)).astype(bf16)
-        kt = keys.T
+
+    def both_heads(first, second, rhs):
+        lhs = jnp.concatenate([first, second], axis=1)
+        return dot(lhs, jnp.concatenate([pick(rhs, 0), pick(rhs, 1)], axis=0)).astype(bf16)
+
+    def products(half, p, i):
+        c = cols(p, 128)
+        do = cot_win[half, :, cols(i, 128)]
+        dkv_win[half, 1, :, c] = both_heads(probs[half, p, 0], probs[half, p, 1], do)
+        dkv_win[half, 0, :, c] = both_heads(ds_s[half, 0], ds_s[half, 1], q_win[half, :, c])
+        kt = kv_win[half, 0, :, c].T
         dq = jnp.concatenate([dot(kt[64 * h : 64 * h + 64], ds_s[half, h]) for h in range(2)], axis=0) * 0.125
         dq_win[half, :, c] = dq.astype(bf16).T[0:BLK]
-        dkv_win[half, 1, :, c] = (dot(probs[half, p, 0], pick(do, 0)) + dot(probs[half, p, 1], pick(do, 1))).astype(bf16)
-        dkv_win[half, 0, :, c] = (dot(ds_s[half, 0], pick(q, 0)) + dot(ds_s[half, 1], pick(q, 1))).astype(bf16)
 
     order = (0, 1, 3, 2)
 
@@ -427,13 +433,13 @@
         return poll
 
     polls = {
-        (0, 0): [sum1_more, w_poll((1, 0), (1, 1))],
+        (0, 0): [w_poll((1, 0), (1, 1))],
         (0, 2): [sum1_mid, w_poll((3, 0), (3, 1))],
         (1, 0): [w_poll((2, 0))],
         (1, 2): [sum2_start],
         (2, 0): [w_poll((2, 1))],
-        (2, 2): [sum2_mid],
-        (3, 1): [sum3_start],
+        (2, 1): [sum2_mid],
+        (3, 0): [sum3_start],
     }
 
     def g_copy(to_next, k, part):
@@ -462,8 +468,11 @@
         if k:
             cotangent(k)
         for part in range(3):
-            for half in range(2):
-                backward(half, ((x + 4 - d) % 4) * 3 + part, part)
+            pair = ((x + 4 - d) % 4) * 3 + part
+            score_grad(0, pair, part)
+            score_grad(1, pair, part)
+            products(0, pair, part)
+            products(1, pair, part)
             if part:
                 g_copy(True, k, part - 1).start()
                 g_copy(False, k, part - 1).start()
@@ -475,8 +484,8 @@
     def _(i):
         c = cols(i, 512)
         w = w_all[:, c]
-        first = dot(att_win[0], w)
-        second = dot(att_win[1], w)
+        both = dot(att_win[...].reshape(2 * BLK, D), w)
+        first, second = both[0:BLK], both[BLK:]
         dout_s[0:192, c] = first[0:192].astype(bf16)
         dout_s[192:208, c] = (first[192:208] + second[0:16]).astype(bf16)
         dout_s[208:392, c] = second[16:200].astype(bf16)

time: 79.2 us -> 77.9 us (0.984); the launches traced: 79.1 us -> 76.5 us
  Pallas kernels: 78.3 us -> 75.7 us
    pallas_call x1, Pallas kernels: 74.4 us -> 71.8 us  [per_device(): pl.pallas_call(kernel, in_specs=[hbm, hbm, hbm, pl.BlockSpec(memory_space...]
where the time goes in v3:
time: 77.9 us; the launch traced here: 76.5 us
  Pallas kernels  75.7 us (97%)
  between operations  0.8 us (1%)
    pallas_call x1, Pallas kernels, per_device(): pl.pallas_call(kernel, in_specs=[hbm, hbm, hbm, pl.BlockSpec(memory_space...  71.8 us
    pallas_call x1, Pallas kernels, per_device(): pl.pallas_call(settle, in_specs=[hbm] * 3, out_specs=[hbm] * 3, out_shape...  3.86 us

profile of v3, /device:TPU:10, one launch (start us, length us, event | category | flops | bytes accessed | tf_op | source)
XLA Modules:
  0.0 76.5 jit_solution(5661180917938485824)
XLA Ops:
  0.6 71.8 %shard_map.67 = (bf16[392,1536]{1,0:T(8,128)(2,1)}, bf16[3,392,1536]{2,1,0:T(8,128)(2,1)}, f32[48,192]{1,0:T(8,128)}) custom-call(bf16[3,392,1536]{2,1,0:T(8,128)(2,1)} %bitcast.4, bf16[192,1536]{1,0:T(8,128)(2,1)} %w_hbm.1, bf16[392,1536]{1,0:T(8,128)(2,1)} %bitcast.5, s32[1,256]{1,0:T(1,128)} %clip_ref.1), custom_call_target="tpu_custom_call" | custom-call | tf_op jit(solution)/shard_map/pallas_call | solution.py:564
  72.4 3.9 %shard_map.68 = (bf16[392,1536]{1,0:T(8,128)(2,1)}, bf16[3,392,1536]{2,1,0:T(8,128)(2,1)}, f32[48,192]{1,0:T(8,128)}) custom-call(bf16[392,1536]{1,0:T(8,128)(2,1)} %get-tuple-element.9.mixed_in, bf16[3,392,1536]{2,1,0:T(8,128)(2,1)} %get-tuple-element.10.grads_in, f32[48,192]{1,0:T(8,128)} %get-tuple-element.11.weight_in), custom_call_target="tpu_custom_call" | custom-call | tf_op jit(solution)/shard_map/pallas_call | solution.py:614
